TPU v7x, 32 devices: a whole 2x2x4 slice. The times are simulated.
32 devices in a mesh: groups: 2 (over y), gx: 4 (over z), gy: 2 (over x), side: 2 (over core).
Axes of the slice: x: 2, y: 2, z: 4, core: 2. Of those that a mesh axis runs over, the one named last changes fastest.
Arguments:
- permeab: float32 [2, 64, 64, 256], P('side', None, 'gx', 'gy'), may hold values from 0.2 to 5
- diffusivity: float32 [2, 64, 64, 256], P('side', None, 'gx', 'gy'), may hold values from 0.2 to 5
- conductivity: float32 [2, 64, 64, 256], P('side', None, 'gx', 'gy'), may hold values from 0.2 to 5
- velocity: float32 [2, 64, 64, 256], P('side', None, 'gx', 'gy'), may hold values from 0.5 to 2
- overpotential: float32 [2, 64, 64, 256], P('side', None, 'gx', 'gy'), may hold values from -3 to 3
- target: float32 [2, 64, 64, 256], P('side', None, 'gx', 'gy'), may hold values from -6 to 6
- inlet_mask: int32 [2, 64, 256], P('side', 'gx', 'gy'), may hold values 0 or 1
- outlet_mask: int32 [2, 64, 256], P('side', 'gx', 'gy'), may hold values 0 or 1
- solid_mask: int32 [4, 64, 64, 256], P(('groups', 'side'), None, 'gx', 'gy'), parts along dimension 0, may hold values 0 or 1
Outputs:
- adjoints: float32 [4, 3, 64, 64, 256], P(('groups', 'side'), None, None, 'gx', 'gy'), parts along dimension 0
There are 2 independent parts, one for each index of `groups`. A program takes and returns all parts, laid end to end along the dimension named above; an argument that names none is the same for every part. Nothing has to cross between parts.
All inputs are finite; a program needn't handle non-finite values. No bound on the sum of `inlet_mask` or of `outlet_mask` or of `solid_mask` on one device may be relied on, other than what follows from the above.
Results may differ from a plain program's by a relative error of at most 0.0001.
Values sent between devices are 32-bit elements; how exact they have to be, the bound alone decides.
A program may use at most 128 MiB of HBM per device.

v0:
```python
import jax
import jax.numpy as jnp
from jax import lax
from jax.sharding import PartitionSpec as P

ITERS = 16


OMEGA = 0.8
MEMBRANE = 1.5


def with_halo(cells, sides, width):
    for axis, dim in sides:
        count = lax.axis_size(axis)
        ends = count - 1
        head = lax.slice_in_dim(cells, 0, width, axis=dim)
        tail = lax.slice_in_dim(cells, cells.shape[dim] - width, cells.shape[dim], axis=dim)
        cells = jnp.concatenate(
            [
                lax.ppermute(tail, axis, [(i, (i + 1) % count) for i in range(ends)]),
                cells,
                lax.ppermute(head, axis, [((i + 1) % count, i) for i in range(ends)]),
            ],
            axis=dim,
        )
    return cells


def swapped(block, axis, stride):
    count = lax.axis_size(axis)
    route = []
    for low in range(count):
        high = low | 1 << stride
        if high != low and high < count:
            route += [(low, high), (high, low)]
    return lax.ppermute(block, axis, route)


def edge_columns(values):
    return jnp.concatenate([values[..., :1], values[..., -1:]], axis=-1)


def shift_columns(values, lower, upper):
    columns = lax.broadcasted_iota(jnp.int32, values.shape, values.ndim - 1)
    final = values.shape[-1] - 1
    forward = jnp.where(columns == final, upper, jnp.roll(values, -1, axis=-1))
    backward = jnp.where(columns == 0, lower, jnp.roll(values, 1, axis=-1))
    return (forward, backward)


def field_columns(values):
    border = with_halo(edge_columns(values), (("gy", 3),), 1)
    return shift_columns(values, border[..., :1], border[..., 3:])


def coef_columns(values):
    border = with_halo(edge_columns(values), (("gy", 3),), 1)
    return shift_columns(values, border[..., :1], border[..., 3:])


def laplace(field_grid, coef, field_next, field_prev, coef_next, coef_prev):
    centre = field_grid[:, 1:-1]
    kcen = coef[:, 1:-1]
    field_depth = jnp.pad(centre, ((1, 1), (0, 0), (0, 0)))
    coef_depth = jnp.pad(kcen, ((1, 1), (0, 0), (0, 0)))
    pairs = (
        (field_grid[:, 2:], coef[:, 2:]),
        (field_grid[:, :-2], coef[:, :-2]),
        (field_next[:, 1:-1], coef_next[:, 1:-1]),
        (field_prev[:, 1:-1], coef_prev[:, 1:-1]),
        (field_depth[2:], coef_depth[2:]),
        (field_depth[:-2], coef_depth[:-2]),
    )
    running_total = jnp.zeros(centre.shape, jnp.float32)
    dsum = jnp.zeros(centre.shape, jnp.float32)
    for neighbour, kneigh in pairs:
        stencil_weight = 0.5 * (kcen + kneigh)
        running_total = running_total + stencil_weight * (neighbour - centre)
        dsum = dsum + stencil_weight
    return (running_total, dsum)


def relax(fields, coefs, field_sides, coef_sides, mirror):
    pres, conc, pot = (fields[0], fields[1], fields[2])
    kperm, kdiff, kcond, speed, rate, inside, blocked, source = [
        coefs[i][:, 1:-1] for i in range(8)
    ]
    field_next, field_prev = field_sides
    coef_next, coef_prev = coef_sides
    lap_p, sum_p = laplace(pres, coefs[0], field_next[0], field_prev[0], coef_next[0], coef_prev[0])
    lap_c, sum_c = laplace(conc, coefs[1], field_next[1], field_prev[1], coef_next[1], coef_prev[1])
    lap_e, sum_e = laplace(pot, coefs[2], field_next[2], field_prev[2], coef_next[2], coef_prev[2])
    pcen = pres[:, 1:-1]
    ccen = conc[:, 1:-1]
    ecen = pot[:, 1:-1]
    ahead = conc[:, 2:] - ccen
    layer = (lax.broadcasted_iota(jnp.int32, pcen.shape, 0) == 0).astype(jnp.float32) * MEMBRANE
    p_new = pcen + OMEGA * (speed * ahead + lap_p - pcen) / (sum_p + 1.0)
    c_new = (
        ccen
        + OMEGA * (source + speed * ahead + lap_c - rate * (ccen - ecen)) / (sum_c + speed + rate)
    ) * (1.0 - blocked)
    e_new = ecen + OMEGA * (lap_e + rate * (ccen - ecen) + layer * (mirror[None] - ecen)) / (
        sum_e + rate + layer
    )
    return jnp.stack([p_new, c_new, e_new]) * inside[None]


def build_coefs(
    permeab,
    diffusivity,
    conductivity,
    velocity,
    overpotential,
    target,
    inlet,
    outlet,
    solid,
    outflow,
    cells,
):
    depth = permeab.shape[0]
    top = (lax.broadcasted_iota(jnp.int32, permeab.shape, 0) == depth - 1).astype(jnp.float32)
    kperm = permeab * (1.0 - 0.95 * solid.astype(jnp.float32))
    rate = 0.5 * (jnp.exp(0.5 * overpotential) + jnp.exp(-0.5 * overpotential))
    blocked = top * inlet.astype(jnp.float32)[None]
    source = target + top * outlet.astype(jnp.float32)[None] * (cells / 8.0) / (1.0 + outflow)
    inside = jnp.ones(permeab.shape, jnp.float32)
    return jnp.stack([kperm, diffusivity, conductivity, velocity, rate, inside, blocked, source])


def advance(extended, coefs, coef_sides):
    mirror = swapped(extended[2, 0, 1:-1], "side", 0)
    field_sides = field_columns(extended)
    return relax(extended, coefs, field_sides, coef_sides, mirror)


def local(
    permeab,
    diffusivity,
    conductivity,
    velocity,
    overpotential,
    target,
    inlet_mask,
    outlet_mask,
    solid_mask,
):
    depth = permeab.shape[1]
    cells = float(permeab.shape[2] * lax.axis_size("gx") * permeab.shape[3] * lax.axis_size("gy"))
    local_flow = jnp.sum(outlet_mask[0].astype(jnp.float32) * velocity[0, depth - 1])
    outflow = lax.psum(local_flow, ("gx", "gy"))
    built = build_coefs(
        permeab[0],
        diffusivity[0],
        conductivity[0],
        velocity[0],
        overpotential[0],
        target[0],
        inlet_mask[0],
        outlet_mask[0],
        solid_mask[0],
        outflow,
        cells,
    )
    wide = with_halo(built, (("gx", 2),), 2)
    wide_next, wide_prev = coef_columns(wide[:3])
    narrow = wide[:, :, 1:-1]
    narrow_sides = (wide_next[:, :, 1:-1], wide_prev[:, :, 1:-1])
    start = jnp.zeros((3,) + permeab.shape[1:], jnp.float32)

    def sweep(step, fields):
        extended = with_halo(fields, (("gx", 2),), 1)
        return advance(extended, narrow, narrow_sides)

    result = lax.fori_loop(0, ITERS, sweep, start)
    return result[None]


def solution(mesh):
    placed = (
        P("side", None, "gx", "gy"),
        P("side", None, "gx", "gy"),
        P("side", None, "gx", "gy"),
        P("side", None, "gx", "gy"),
        P("side", None, "gx", "gy"),
        P("side", None, "gx", "gy"),
        P("side", "gx", "gy"),
        P("side", "gx", "gy"),
        P(("groups", "side"), None, "gx", "gy"),
    )
    return jax.shard_map(
        local,
        mesh=mesh,
        in_specs=placed,
        out_specs=P(("groups", "side"), None, None, "gx", "gy"),
        check_vma=False,
    )
```

profile of v0, /device:TPU:0, one launch (start us, length us, event | category | flops | bytes accessed | tf_op | source)
XLA Modules:
  0.0 1118.9 jit_solution(11155834878441740167)
XLA Ops:
  2.1 23.7 %psum.7 = f32[]{:T(128)} all-reduce(f32[]{:T(128)} %fusion.49), channel_id=1, replica_groups=mesh['groups'=2,'gx'=4,'gy'=2,'side'=2] {'gx','gy'}, use_global_device_ids=true, to_apply=%region_1.0 | all-reduce | flops 1 | bytes 8 | tf_op jit(solution)/shard_map/psum | solution.py:153
  42.5 6.3 collective-permute-done.5
  76.8 8.7 copy.103
  113.5 1002.2 %while.13 = (s32[]{:T(128)}, f32[3,64,16,128]{1,2,3,0:T(8,128)}, f32[8,64,18,128]{1,2,3,0:T(8,128)}, f32[64,16,128]{0,1,2:T(8,128)}, f32[64,16,128]{0,1,2:T(8,12...) while((s32[]{:T(128)}, f32[3,64,16,128]{1,2,3,0:T(8,128)}, ...), condition=%wide.region_3.4_spmd.clone, body=%wide.region_2.3_spmd.clone.sunk | while | flops 20232068 | bytes 123359384 | solution.py:177
  124.4 9.3 slice_bitcast_fusion.26
  157.2 5.3 fusion.62
  186.1 9.3 slice_bitcast_fusion.26
  220.0 5.3 fusion.62
  249.0 9.3 slice_bitcast_fusion.26
  282.8 5.3 fusion.62
  311.8 9.3 slice_bitcast_fusion.26
  345.6 5.3 fusion.62
  374.6 9.3 slice_bitcast_fusion.26
  437.4 9.3 slice_bitcast_fusion.26
  500.3 9.3 slice_bitcast_fusion.26
  563.1 9.3 slice_bitcast_fusion.26
  625.9 9.3 slice_bitcast_fusion.26
  688.7 9.3 slice_bitcast_fusion.26
  751.5 9.3 slice_bitcast_fusion.26
  814.4 9.3 slice_bitcast_fusion.26
  877.2 9.3 slice_bitcast_fusion.26
  940.0 9.3 slice_bitcast_fusion.26
  1002.8 9.3 slice_bitcast_fusion.26
  1065.7 9.3 slice_bitcast_fusion.26
  (1489 shorter events, 903.7 us)
Async XLA Ops:
  114.8 27.6 %collective-permute-start = (f32[3,64,1,128]{1,2,3,0:T(1,128)}, f32[3,64,1,128]{1,2,3,0:T(1,128)S(1)}, u32[]{:S(2)}, u32[]{:S(2)}) collective-permute-start(f32[3,64,1,128]{1,2,3,0:T(1,128)} %get-tuple-element.414), channel_id=1, source_target_pairs={{4,0},{8,4},{12,8},{5,1},{9,5},{13,9},{6,2},{10,6},{14,10},{7,3},{... | collective-permute-start | bytes 294920 | tf_op jit(solution)/shard_map/while/body/eval_jaxpr/ppermute | solution.py:23
  116.1 26.3 %collective-permute-start.1 = (f32[3,64,1,128]{1,2,3,0:T(1,128)}, f32[3,64,1,128]{1,2,3,0:T(1,128)S(1)}, u32[]{:S(2)}, u32[]{:S(2)}) collective-permute-start(f32[3,64,1,128]{1,2,3,0:T(1,128)} %get-tuple-element.415), channel_id=1, source_target_pairs={{0,4},{4,8},{8,12},{1,5},{5,9},{9,13},{2,6},{6,10},{10,14},{3,7},{... | collective-permute-start | bytes 294920 | tf_op jit(solution)/shard_map/while/body/eval_jaxpr/ppermute | solution.py:21
  176.5 27.6 %collective-permute-start = (f32[3,64,1,128]{1,2,3,0:T(1,128)}, f32[3,64,1,128]{1,2,3,0:T(1,128)S(1)}, u32[]{:S(2)}, u32[]{:S(2)}) collective-permute-start(f32[3,64,1,128]{1,2,3,0:T(1,128)} %get-tuple-element.414), channel_id=1, source_target_pairs={{4,0},{8,4},{12,8},{5,1},{9,5},{13,9},{6,2},{10,6},{14,10},{7,3},{... | collective-permute-start | bytes 294920 | tf_op jit(solution)/shard_map/while/body/eval_jaxpr/ppermute | solution.py:23
  239.4 27.6 %collective-permute-start = (f32[3,64,1,128]{1,2,3,0:T(1,128)}, f32[3,64,1,128]{1,2,3,0:T(1,128)S(1)}, u32[]{:S(2)}, u32[]{:S(2)}) collective-permute-start(f32[3,64,1,128]{1,2,3,0:T(1,128)} %get-tuple-element.414), channel_id=1, source_target_pairs={{4,0},{8,4},{12,8},{5,1},{9,5},{13,9},{6,2},{10,6},{14,10},{7,3},{... | collective-permute-start | bytes 294920 | tf_op jit(solution)/shard_map/while/body/eval_jaxpr/ppermute | solution.py:23
  240.6 26.3 %collective-permute-start.1 = (f32[3,64,1,128]{1,2,3,0:T(1,128)}, f32[3,64,1,128]{1,2,3,0:T(1,128)S(1)}, u32[]{:S(2)}, u32[]{:S(2)}) collective-permute-start(f32[3,64,1,128]{1,2,3,0:T(1,128)} %get-tuple-element.415), channel_id=1, source_target_pairs={{0,4},{4,8},{8,12},{1,5},{5,9},{9,13},{2,6},{6,10},{10,14},{3,7},{... | collective-permute-start | bytes 294920 | tf_op jit(solution)/shard_map/while/body/eval_jaxpr/ppermute | solution.py:21
  302.2 27.6 %collective-permute-start = (f32[3,64,1,128]{1,2,3,0:T(1,128)}, f32[3,64,1,128]{1,2,3,0:T(1,128)S(1)}, u32[]{:S(2)}, u32[]{:S(2)}) collective-permute-start(f32[3,64,1,128]{1,2,3,0:T(1,128)} %get-tuple-element.414), channel_id=1, source_target_pairs={{4,0},{8,4},{12,8},{5,1},{9,5},{13,9},{6,2},{10,6},{14,10},{7,3},{... | collective-permute-start | bytes 294920 | tf_op jit(solution)/shard_map/while/body/eval_jaxpr/ppermute | solution.py:23
  303.5 26.3 %collective-permute-start.1 = (f32[3,64,1,128]{1,2,3,0:T(1,128)}, f32[3,64,1,128]{1,2,3,0:T(1,128)S(1)}, u32[]{:S(2)}, u32[]{:S(2)}) collective-permute-start(f32[3,64,1,128]{1,2,3,0:T(1,128)} %get-tuple-element.415), channel_id=1, source_target_pairs={{0,4},{4,8},{8,12},{1,5},{5,9},{9,13},{2,6},{6,10},{10,14},{3,7},{... | collective-permute-start | bytes 294920 | tf_op jit(solution)/shard_map/while/body/eval_jaxpr/ppermute | solution.py:21
  365.0 27.6 %collective-permute-start = (f32[3,64,1,128]{1,2,3,0:T(1,128)}, f32[3,64,1,128]{1,2,3,0:T(1,128)S(1)}, u32[]{:S(2)}, u32[]{:S(2)}) collective-permute-start(f32[3,64,1,128]{1,2,3,0:T(1,128)} %get-tuple-element.414), channel_id=1, source_target_pairs={{4,0},{8,4},{12,8},{5,1},{9,5},{13,9},{6,2},{10,6},{14,10},{7,3},{... | collective-permute-start | bytes 294920 | tf_op jit(solution)/shard_map/while/body/eval_jaxpr/ppermute | solution.py:23
  366.3 26.3 %collective-permute-start.1 = (f32[3,64,1,128]{1,2,3,0:T(1,128)}, f32[3,64,1,128]{1,2,3,0:T(1,128)S(1)}, u32[]{:S(2)}, u32[]{:S(2)}) collective-permute-start(f32[3,64,1,128]{1,2,3,0:T(1,128)} %get-tuple-element.415), channel_id=1, source_target_pairs={{0,4},{4,8},{8,12},{1,5},{5,9},{9,13},{2,6},{6,10},{10,14},{3,7},{... | collective-permute-start | bytes 294920 | tf_op jit(solution)/shard_map/while/body/eval_jaxpr/ppermute | solution.py:21
  427.8 27.6 %collective-permute-start = (f32[3,64,1,128]{1,2,3,0:T(1,128)}, f32[3,64,1,128]{1,2,3,0:T(1,128)S(1)}, u32[]{:S(2)}, u32[]{:S(2)}) collective-permute-start(f32[3,64,1,128]{1,2,3,0:T(1,128)} %get-tuple-element.414), channel_id=1, source_target_pairs={{4,0},{8,4},{12,8},{5,1},{9,5},{13,9},{6,2},{10,6},{14,10},{7,3},{... | collective-permute-start | bytes 294920 | tf_op jit(solution)/shard_map/while/body/eval_jaxpr/ppermute | solution.py:23
  490.6 27.6 %collective-permute-start = (f32[3,64,1,128]{1,2,3,0:T(1,128)}, f32[3,64,1,128]{1,2,3,0:T(1,128)S(1)}, u32[]{:S(2)}, u32[]{:S(2)}) collective-permute-start(f32[3,64,1,128]{1,2,3,0:T(1,128)} %get-tuple-element.414), channel_id=1, source_target_pairs={{4,0},{8,4},{12,8},{5,1},{9,5},{13,9},{6,2},{10,6},{14,10},{7,3},{... | collective-permute-start | bytes 294920 | tf_op jit(solution)/shard_map/while/body/eval_jaxpr/ppermute | solution.py:23
  491.9 26.3 %collective-permute-start.1 = (f32[3,64,1,128]{1,2,3,0:T(1,128)}, f32[3,64,1,128]{1,2,3,0:T(1,128)S(1)}, u32[]{:S(2)}, u32[]{:S(2)}) collective-permute-start(f32[3,64,1,128]{1,2,3,0:T(1,128)} %get-tuple-element.415), channel_id=1, source_target_pairs={{0,4},{4,8},{8,12},{1,5},{5,9},{9,13},{2,6},{6,10},{10,14},{3,7},{... | collective-permute-start | bytes 294920 | tf_op jit(solution)/shard_map/while/body/eval_jaxpr/ppermute | solution.py:21
  553.5 27.6 %collective-permute-start = (f32[3,64,1,128]{1,2,3,0:T(1,128)}, f32[3,64,1,128]{1,2,3,0:T(1,128)S(1)}, u32[]{:S(2)}, u32[]{:S(2)}) collective-permute-start(f32[3,64,1,128]{1,2,3,0:T(1,128)} %get-tuple-element.414), channel_id=1, source_target_pairs={{4,0},{8,4},{12,8},{5,1},{9,5},{13,9},{6,2},{10,6},{14,10},{7,3},{... | collective-permute-start | bytes 294920 | tf_op jit(solution)/shard_map/while/body/eval_jaxpr/ppermute | solution.py:23
  554.8 26.3 %collective-permute-start.1 = (f32[3,64,1,128]{1,2,3,0:T(1,128)}, f32[3,64,1,128]{1,2,3,0:T(1,128)S(1)}, u32[]{:S(2)}, u32[]{:S(2)}) collective-permute-start(f32[3,64,1,128]{1,2,3,0:T(1,128)} %get-tuple-element.415), channel_id=1, source_target_pairs={{0,4},{4,8},{8,12},{1,5},{5,9},{9,13},{2,6},{6,10},{10,14},{3,7},{... | collective-permute-start | bytes 294920 | tf_op jit(solution)/shard_map/while/body/eval_jaxpr/ppermute | solution.py:21
  616.3 27.6 %collective-permute-start = (f32[3,64,1,128]{1,2,3,0:T(1,128)}, f32[3,64,1,128]{1,2,3,0:T(1,128)S(1)}, u32[]{:S(2)}, u32[]{:S(2)}) collective-permute-start(f32[3,64,1,128]{1,2,3,0:T(1,128)} %get-tuple-element.414), channel_id=1, source_target_pairs={{4,0},{8,4},{12,8},{5,1},{9,5},{13,9},{6,2},{10,6},{14,10},{7,3},{... | collective-permute-start | bytes 294920 | tf_op jit(solution)/shard_map/while/body/eval_jaxpr/ppermute | solution.py:23
  617.6 26.3 %collective-permute-start.1 = (f32[3,64,1,128]{1,2,3,0:T(1,128)}, f32[3,64,1,128]{1,2,3,0:T(1,128)S(1)}, u32[]{:S(2)}, u32[]{:S(2)}) collective-permute-start(f32[3,64,1,128]{1,2,3,0:T(1,128)} %get-tuple-element.415), channel_id=1, source_target_pairs={{0,4},{4,8},{8,12},{1,5},{5,9},{9,13},{2,6},{6,10},{10,14},{3,7},{... | collective-permute-start | bytes 294920 | tf_op jit(solution)/shard_map/while/body/eval_jaxpr/ppermute | solution.py:21
  679.1 27.6 %collective-permute-start = (f32[3,64,1,128]{1,2,3,0:T(1,128)}, f32[3,64,1,128]{1,2,3,0:T(1,128)S(1)}, u32[]{:S(2)}, u32[]{:S(2)}) collective-permute-start(f32[3,64,1,128]{1,2,3,0:T(1,128)} %get-tuple-element.414), channel_id=1, source_target_pairs={{4,0},{8,4},{12,8},{5,1},{9,5},{13,9},{6,2},{10,6},{14,10},{7,3},{... | collective-permute-start | bytes 294920 | tf_op jit(solution)/shard_map/while/body/eval_jaxpr/ppermute | solution.py:23
  680.4 26.3 %collective-permute-start.1 = (f32[3,64,1,128]{1,2,3,0:T(1,128)}, f32[3,64,1,128]{1,2,3,0:T(1,128)S(1)}, u32[]{:S(2)}, u32[]{:S(2)}) collective-permute-start(f32[3,64,1,128]{1,2,3,0:T(1,128)} %get-tuple-element.415), channel_id=1, source_target_pairs={{0,4},{4,8},{8,12},{1,5},{5,9},{9,13},{2,6},{6,10},{10,14},{3,7},{... | collective-permute-start | bytes 294920 | tf_op jit(solution)/shard_map/while/body/eval_jaxpr/ppermute | solution.py:21
  741.9 27.6 %collective-permute-start = (f32[3,64,1,128]{1,2,3,0:T(1,128)}, f32[3,64,1,128]{1,2,3,0:T(1,128)S(1)}, u32[]{:S(2)}, u32[]{:S(2)}) collective-permute-start(f32[3,64,1,128]{1,2,3,0:T(1,128)} %get-tuple-element.414), channel_id=1, source_target_pairs={{4,0},{8,4},{12,8},{5,1},{9,5},{13,9},{6,2},{10,6},{14,10},{7,3},{... | collective-permute-start | bytes 294920 | tf_op jit(solution)/shard_map/while/body/eval_jaxpr/ppermute | solution.py:23
  804.8 27.6 %collective-permute-start = (f32[3,64,1,128]{1,2,3,0:T(1,128)}, f32[3,64,1,128]{1,2,3,0:T(1,128)S(1)}, u32[]{:S(2)}, u32[]{:S(2)}) collective-permute-start(f32[3,64,1,128]{1,2,3,0:T(1,128)} %get-tuple-element.414), channel_id=1, source_target_pairs={{4,0},{8,4},{12,8},{5,1},{9,5},{13,9},{6,2},{10,6},{14,10},{7,3},{... | collective-permute-start | bytes 294920 | tf_op jit(solution)/shard_map/while/body/eval_jaxpr/ppermute | solution.py:23
  867.6 27.6 %collective-permute-start = (f32[3,64,1,128]{1,2,3,0:T(1,128)}, f32[3,64,1,128]{1,2,3,0:T(1,128)S(1)}, u32[]{:S(2)}, u32[]{:S(2)}) collective-permute-start(f32[3,64,1,128]{1,2,3,0:T(1,128)} %get-tuple-element.414), channel_id=1, source_target_pairs={{4,0},{8,4},{12,8},{5,1},{9,5},{13,9},{6,2},{10,6},{14,10},{7,3},{... | collective-permute-start | bytes 294920 | tf_op jit(solution)/shard_map/while/body/eval_jaxpr/ppermute | solution.py:23
  930.4 27.6 %collective-permute-start = (f32[3,64,1,128]{1,2,3,0:T(1,128)}, f32[3,64,1,128]{1,2,3,0:T(1,128)S(1)}, u32[]{:S(2)}, u32[]{:S(2)}) collective-permute-start(f32[3,64,1,128]{1,2,3,0:T(1,128)} %get-tuple-element.414), channel_id=1, source_target_pairs={{4,0},{8,4},{12,8},{5,1},{9,5},{13,9},{6,2},{10,6},{14,10},{7,3},{... | collective-permute-start | bytes 294920 | tf_op jit(solution)/shard_map/while/body/eval_jaxpr/ppermute | solution.py:23
  993.2 27.6 %collective-permute-start = (f32[3,64,1,128]{1,2,3,0:T(1,128)}, f32[3,64,1,128]{1,2,3,0:T(1,128)S(1)}, u32[]{:S(2)}, u32[]{:S(2)}) collective-permute-start(f32[3,64,1,128]{1,2,3,0:T(1,128)} %get-tuple-element.414), channel_id=1, source_target_pairs={{4,0},{8,4},{12,8},{5,1},{9,5},{13,9},{6,2},{10,6},{14,10},{7,3},{... | collective-permute-start | bytes 294920 | tf_op jit(solution)/shard_map/while/body/eval_jaxpr/ppermute | solution.py:23
  1056.0 27.6 %collective-permute-start = (f32[3,64,1,128]{1,2,3,0:T(1,128)}, f32[3,64,1,128]{1,2,3,0:T(1,128)S(1)}, u32[]{:S(2)}, u32[]{:S(2)}) collective-permute-start(f32[3,64,1,128]{1,2,3,0:T(1,128)} %get-tuple-element.414), channel_id=1, source_target_pairs={{4,0},{8,4},{12,8},{5,1},{9,5},{13,9},{6,2},{10,6},{14,10},{7,3},{... | collective-permute-start | bytes 294920 | tf_op jit(solution)/shard_map/while/body/eval_jaxpr/ppermute | solution.py:23
  (510 other events, 2920.7 us)
where the time goes:
time: 1120 us
  local copies, waits for them, and re-layouts  527 us (47%)
  other arithmetic  346 us (31%)
  starting transfers between devices  170 us (15%)
  waiting for transfers between devices  45.5 us (4%)
  blocking collectives  23.7 us (2%)
    another operation x48, other arithmetic, relax(): return jnp.stack([p_new, c_new, e_new]) * inside[None]  183 us
    squeeze x16, local copies, waits for them, and re-layouts, relax(): coefs[i][:, 1:-1]  149 us
    ppermute x34, starting transfers between devices, with_halo(): lax.ppermute(tail, axis, [(i, (i + 1) % count) for i in range(ends)])  126 us
    slice x48, local copies, waits for them, and re-layouts, laplace(): kcen = coef[:, 1:-1]  100 us
    squeeze x16, local copies, waits for them, and re-layouts, relax(): field_prev[0]  62.2 us
    ppermute x34, starting transfers between devices, with_halo(): lax.ppermute(head, axis, [((i + 1) % count, i) for i in range(ends)])  44 us
    while x864, local copies, waits for them, and re-layouts  43.8 us
    slice x32, local copies, waits for them, and re-layouts, advance(): mirror = swapped(extended[2, 0, 1:-1], 'side', 0)  42.7 us
  transfers between devices with their start and end apart: 84, of which 18 were waited for; matrix products, arithmetic and copies ran while one was open for 39% of the time, Pallas kernels for 0%

commit v1 on v0

v1 whole, which is shorter than its diff:
```python
import functools

import jax
import jax.numpy as jnp
from jax import lax
from jax.experimental import pallas as pl
from jax.experimental.pallas import tpu as pltpu
from jax.sharding import PartitionSpec as P

ITERS = 16
OMEGA = 0.8
MEMBRANE = 1.5
CHUNKS = 4
MESH = pl.DeviceIdType.MESH
f32 = jnp.float32


def kernel(
    ngx, ngy, depth,
    permeab, diffusivity, conductivity, velocity, overpotential, target, inlet, outlet, solid,
    out,
    F, W, sx, hx, sy, hy, keep, extra, part, got_x, got_y,
    send_sem, recv_sem, flow_send, flow_recv,
):
    zc = depth // CHUNKS
    gx, gy, side = lax.axis_index("gx"), lax.axis_index("gy"), lax.axis_index("side")
    cells = float(16 * ngx * 128 * ngy)
    lane = lax.broadcasted_iota(jnp.int32, (8, 128), 1)
    sub = lax.broadcasted_iota(jnp.int32, (8, 128), 0)
    first_lane, last_lane = lane == 0, lane == 127
    first_row, last_row = sub == 0, sub == 7
    pair = lane // 2
    even = lane % 2 == 0
    zero = jnp.zeros((8, 128), f32)

    for p in range(2):
        for f in range(3):
            F[p, f, 0] = jnp.zeros((32, 128), f32)
            F[p, f, depth + 1] = jnp.zeros((32, 128), f32)
    hx[...] = jnp.zeros(hx.shape, f32)
    hy[...] = jnp.zeros(hy.shape, f32)

    barrier = pltpu.get_barrier_semaphore()
    for d in range(1, ngx):
        pl.semaphore_signal(barrier, inc=1, device_id={"gx": lax.rem(gx + d, ngx)}, device_id_type=MESH)
    for d in range(1, ngy):
        pl.semaphore_signal(barrier, inc=1, device_id={"gy": lax.rem(gy + d, ngy)}, device_id_type=MESH)
    pl.semaphore_signal(barrier, inc=1, device_id={"side": 1 - side}, device_id_type=MESH)
    pl.semaphore_wait(barrier, ngx - 1 + ngy - 1 + 1)

    def flow_copy(axis, me, count, d, src, dst, sending):
        k = 0 if axis == "gx" else 1
        peer = lax.rem(me + d, count) if sending else lax.rem(me + count - d, count)
        slot = me if sending else peer
        return pltpu.make_async_remote_copy(
            src_ref=src, dst_ref=dst.at[slot],
            send_sem=flow_send.at[k, d], recv_sem=flow_recv.at[k, d],
            device_id={axis: peer}, device_id_type=MESH,
        )

    tile = zero
    for h in range(2):
        rows = pl.ds(8 * h, 8)
        tile = tile + outlet[0, rows].astype(f32) * velocity[0, depth - 1, rows]
    part[0] = tile
    for d in range(1, ngx):
        flow_copy("gx", gx, ngx, d, part.at[0], got_x, True).start()

    has_lower = (gx > 0, gy > 0)
    has_upper = (gx < ngx - 1, gy < ngy - 1)
    can_send = (has_upper[0], has_lower[0], has_upper[1], has_lower[1])
    can_recv = (has_lower[0], has_upper[0], has_lower[1], has_upper[1])

    def halo_copy(p, d, c):
        if d == 4:
            src, dst = F.at[p, 2, 1, pl.ds(8, 16)], F.at[p, 2, 0, pl.ds(8, 16)]
            where = {"side": 1 - side}
        elif d < 2:
            src, dst = sx.at[p, 1 - d, c], hx.at[p, d, c]
            where = {"gx": gx + 1 if d == 0 else gx - 1}
        else:
            src, dst = sy.at[p, c], hy.at[p, d - 2, c]
            where = {"gy": gy + 1 if d == 2 else gy - 1}
        return pltpu.make_async_remote_copy(
            src_ref=src, dst_ref=dst,
            send_sem=send_sem.at[p, d, c], recv_sem=recv_sem.at[p, d, c],
            device_id=where, device_id_type=MESH,
        )

    def send(p, c, membrane):
        for d in range(4):
            @pl.when(can_send[d])
            def _(d=d):
                halo_copy(p, d, c).start()
        if membrane and c == 0:
            halo_copy(p, 4, c).start()

    def receive(p, c, membrane):
        for d in range(4):
            @pl.when(can_send[d])
            def _(d=d):
                halo_copy(p, d, c).wait_send()

            @pl.when(can_recv[d])
            def _(d=d):
                halo_copy(p, d, c).wait_recv()
        if membrane and c == 0:
            copy = halo_copy(p, 4, c)
            copy.wait_send()
            copy.wait_recv()

    def columns(p, c):
        lists = []
        for f in range(3):
            upper, lower = hy[p, 1, c, f], hy[p, 0, c, f]
            lists.append(jnp.where(even, pltpu.roll(upper, 127, 1), pltpu.roll(lower, 1, 1)))
        return lists

    def around(p, c, f, iz, h, cols):
        at = c * zc + iz + 1
        r = 8 + 8 * h
        cen = F[p, f, at, pl.ds(r, 8)]
        below = F[p, f, at - 1, pl.ds(r, 8)]
        above = F[p, f, at + 1, pl.ds(r, 8)]
        xm = F[p, f, at, pl.ds(r - 1, 8)]
        xp = F[p, f, at, pl.ds(r + 1, 8)]
        if h == 0:
            xm = jnp.where(first_row, jnp.broadcast_to(hx[p, 0, c, f, pl.ds(iz, 1)], (8, 128)), xm)
        else:
            xp = jnp.where(last_row, jnp.broadcast_to(hx[p, 1, c, f, pl.ds(iz, 1)], (8, 128)), xp)
        spot = 2 * (2 * iz + h) + 1
        side_cols = pltpu.roll(cols[f], 128 - spot, 1)
        ym = jnp.where(first_lane, side_cols, pltpu.roll(cen, 1, 1))
        yp = jnp.where(last_lane, side_cols, pltpu.roll(cen, 127, 1))
        return cen, (below, above, xm, xp, ym, yp)

    def put(q, c, f, iz, h, value, packed):
        F[q, f, c * zc + iz + 1, pl.ds(8 + 8 * h, 8)] = value
        if h == 0:
            sx[q, 0, c, f, pl.ds(iz, 1)] = value[0:1]
        else:
            sx[q, 1, c, f, pl.ds(iz, 1)] = value[7:8]
        ti = 2 * iz + h
        return jnp.where(pair == ti, pltpu.roll(value, 2 * ti + 1, 1), packed)

    def chunk_of(q, c, plane, unroll, store=True):
        def body(i, packed):
            packed = list(packed)
            for u in range(unroll):
                iz = i * unroll + u
                for h in range(2):
                    values = plane(iz, h)
                    if store:
                        for f in range(3):
                            packed[f] = put(q, c, f, iz, h, values[f], packed[f])
            return tuple(packed)

        packed = lax.fori_loop(0, zc // unroll, body, (zero, zero, zero))
        if store:
            for f in range(3):
                sy[q, c, f] = packed[f]

    for c in range(CHUNKS):
        def plane(iz, h, c=c):
            z, rows = c * zc + iz, pl.ds(8 * h, 8)
            kp = permeab[0, z, rows] * (1.0 - 0.95 * solid[0, z, rows].astype(f32))
            return kp, diffusivity[0, z, rows], conductivity[0, z, rows]

        chunk_of(0, c, plane, 2)
        send(0, c, False)

    for h in range(2):
        rows = pl.ds(8 * h, 8)
        keep[0, rows] = jnp.full((8, 128), 1.0 - OMEGA, f32)
        keep[1, rows] = (1.0 - OMEGA) * (1.0 - inlet[0, rows].astype(f32))
        extra[rows] = zero

    for c in range(CHUNKS):
        if c == 0 and CHUNKS > 1:
            total = part[0]
            for d in range(1, ngx):
                flow_copy("gx", gx, ngx, d, part.at[0], got_x, True).wait_send()
                flow_copy("gx", gx, ngx, d, part.at[0], got_x, False).wait_recv()
                total = total + got_x[lax.rem(gx + ngx - d, ngx)]
            part[1] = total
            for d in range(1, ngy):
                flow_copy("gy", gy, ngy, d, part.at[1], got_y, True).start()
        if c == CHUNKS - 1:
            total = part[1]
            for d in range(1, ngy):
                flow_copy("gy", gy, ngy, d, part.at[1], got_y, True).wait_send()
                flow_copy("gy", gy, ngy, d, part.at[1], got_y, False).wait_recv()
                total = total + got_y[lax.rem(gy + ngy - d, ngy)]
            outflow = jnp.sum(jnp.sum(total, axis=0, keepdims=True), axis=1, keepdims=True)
            scale = jnp.broadcast_to((cells / 8.0) / (1.0 + outflow), (8, 128))
            for h in range(2):
                rows = pl.ds(8 * h, 8)
                extra[rows] = outlet[0, rows].astype(f32) * scale
        receive(0, c, False)
        cols = columns(0, c)

        def plane(iz, h, c=c, cols=cols):
            z, rows = c * zc + iz, pl.ds(8 * h, 8)
            bottom = (z == 0).astype(f32)
            top = (z == depth - 1).astype(f32)
            vel = velocity[0, z, rows]
            half = 0.5 * overpotential[0, z, rows]
            rate = 0.5 * (jnp.exp(half) + jnp.exp(-half))
            g = jnp.full((8, 128), MEMBRANE, f32) * bottom
            source = target[0, z, rows] + top * extra[rows]
            free = 1.0 - top * inlet[0, rows].astype(f32)
            for f, base in ((0, 0), (1, 7), (2, 15)):
                cen, near = around(0, c, f, iz, h, cols)
                w = [0.5 * (cen + k) for k in near]
                dsum = ((w[0] + w[1]) + (w[2] + w[3])) + (w[4] + w[5])
                if f == 0:
                    factor = OMEGA / (dsum + 1.0)
                    W[6, z, rows] = factor * vel
                elif f == 1:
                    factor = OMEGA * free / (dsum + vel + rate)
                    w[3] = w[3] + vel
                    start = factor * source
                    W[13, z, rows] = start
                    W[14, z, rows] = factor * rate
                else:
                    factor = OMEGA / (dsum + rate + g)
                    w[0] = w[0] * (1.0 - bottom) + g
                    W[21, z, rows] = factor * rate
                for n in range(6):
                    W[base + n, z, rows] = factor * w[n]
            return zero, start, zero

        chunk_of(1, c, plane, 2)
        send(1, c, True)

    def sweep_chunk(p, q, c, final):
        receive(p, c, True)
        cols = columns(p, c)

        def plane(iz, h):
            z, rows = c * zc + iz, pl.ds(8 * h, 8)
            top = (z == depth - 1).astype(jnp.int32)

            def mixed(base, near):
                t = [W[base + n, z, rows] * near[n] for n in range(6)]
                return ((t[0] + t[1]) + (t[2] + t[3])) + (t[4] + t[5])

            pc, pn = around(p, c, 0, iz, h, cols)
            cc, cn = around(p, c, 1, iz, h, cols)
            ec, en = around(p, c, 2, iz, h, cols)
            p_new = mixed(0, pn) + ((1.0 - OMEGA) * pc + W[6, z, rows] * (cn[3] - cc))
            c_new = mixed(7, cn) + (keep[top, rows] * cc + (W[13, z, rows] + W[14, z, rows] * ec))
            e_new = mixed(15, en) + ((1.0 - OMEGA) * ec + W[21, z, rows] * cc)
            if final:
                out[0, 0, z, rows] = p_new
                out[0, 1, z, rows] = c_new
                out[0, 2, z, rows] = e_new
            return p_new, c_new, e_new

        chunk_of(q, c, plane, 2, not final)
        if not final:
            send(q, c, True)

    def sweep(t, carry):
        p = lax.rem(t, 2)
        for c in range(CHUNKS):
            sweep_chunk(p, 1 - p, c, False)
        return carry

    lax.fori_loop(1, ITERS - 1, sweep, 0)
    last = (ITERS - 1) % 2
    for c in range(CHUNKS):
        sweep_chunk(last, 1 - last, c, True)


def solution(mesh):
    ngx, ngy = mesh.shape["gx"], mesh.shape["gy"]

    def local(*args):
        depth = args[0].shape[1]
        zc = depth // CHUNKS
        vmem = pl.BlockSpec(memory_space=pltpu.VMEM)
        return pl.pallas_call(
            functools.partial(kernel, ngx, ngy, depth),
            out_shape=jax.ShapeDtypeStruct((1, 3, depth, 16, 128), f32),
            in_specs=[vmem] * 9,
            out_specs=vmem,
            scratch_shapes=[
                pltpu.VMEM((2, 3, depth + 2, 32, 128), f32),
                pltpu.VMEM((22, depth, 16, 128), f32),
                pltpu.VMEM((2, 2, CHUNKS, 3, zc, 128), f32),
                pltpu.VMEM((2, 2, CHUNKS, 3, zc, 128), f32),
                pltpu.VMEM((2, CHUNKS, 3, 8, 128), f32),
                pltpu.VMEM((2, 2, CHUNKS, 3, 8, 128), f32),
                pltpu.VMEM((2, 16, 128), f32),
                pltpu.VMEM((16, 128), f32),
                pltpu.VMEM((2, 8, 128), f32),
                pltpu.VMEM((ngx, 8, 128), f32),
                pltpu.VMEM((ngy, 8, 128), f32),
                pltpu.SemaphoreType.DMA((2, 5, CHUNKS)),
                pltpu.SemaphoreType.DMA((2, 5, CHUNKS)),
                pltpu.SemaphoreType.DMA((2, max(ngx, ngy))),
                pltpu.SemaphoreType.DMA((2, max(ngx, ngy))),
            ],
            compiler_params=pltpu.CompilerParams(
                collective_id=0, has_side_effects=True, vmem_limit_bytes=48 * 1024 * 1024
            ),
        )(*args)

    placed = (
        (P("side", None, "gx", "gy"),) * 6
        + (P("side", "gx", "gy"),) * 2
        + (P(("groups", "side"), None, "gx", "gy"),)
    )
    return jax.shard_map(
        local,
        mesh=mesh,
        in_specs=placed,
        out_specs=P(("groups", "side"), None, None, "gx", "gy"),
        check_vma=False,
    )
```

time: 1120 us -> 205 us (0.18)
  local copies, waits for them, and re-layouts: 527 us -> 9.83 us
  other arithmetic: 346 us -> 0 us
  Pallas kernels: 0 us -> 195 us
  starting transfers between devices: 170 us -> 0 us
  waiting for transfers between devices: 45.5 us -> 0 us
  blocking collectives: 23.7 us -> 0 us
    squeeze x50 -> x0, local copies, waits for them, and re-layouts: 218 us -> none  [the longest x16 149 us: relax(): coefs[i][:, 1:-1]]
    slice x148 -> x0, local copies, waits for them, and re-layouts: 213 us -> none  [the longest x48 100 us: laplace(): kcen = coef[:, 1:-1]]
    pallas_call x0 -> x1, Pallas kernels: none -> 195 us  [local(): pl.pallas_call(functools.partial(kernel, ngx, ngy, depth), out_shape=jax....]
    another operation x49 -> x0, other arithmetic: 184 us -> none  [the longest x48 183 us: relax(): return jnp.stack([p_new, c_new, e_new]) * inside[None]]
    ppermute x84 -> x0, starting transfers between devices: 170 us -> none  [the longest x34 126 us: with_halo(): lax.ppermute(tail, axis, [(i, (i + 1) % count) for i in range(ends)])]
    while x865 -> x0, local copies, waits for them, and re-layouts: 47 us -> none
    ppermute x84 -> x0, waiting for transfers between devices: 45.5 us -> none  [the longest x34 39 us: with_halo(): lax.ppermute(head, axis, [((i + 1) % count, i) for i in range(ends)])]
    mul x34 -> x0, other arithmetic: 41.2 us -> none  [the longest x16 31.5 us: relax(): return jnp.stack([p_new, c_new, e_new]) * inside[None]]
  transfers between devices with their start and end apart: 84 -> 0, of which waited for: 18 -> 0; matrix products, arithmetic and copies ran while one was open for 39% -> 0% of each run, Pallas kernels for 0% -> 0%
where the time goes in v1:
time: 205 us
  Pallas kernels  195 us (95%)
  local copies, waits for them, and re-layouts  9.83 us (5%)
    pallas_call x1, Pallas kernels, local(): pl.pallas_call(functools.partial(kernel, ngx, ngy, depth), out_shape=jax....  195 us
    unnamed x19, local copies, waits for them, and re-layouts  9.83 us

profile of v1, /device:TPU:0, one launch (start us, length us, event | category | flops | bytes accessed | tf_op | source)
XLA Modules:
  0.0 204.8 jit_solution(6269721405082698495)
XLA Ops:
  0.0 0.0 copy-start
  0.0 1.0 copy-done
  1.0 0.0 copy-start.1
  1.0 1.0 copy-done.1
  2.1 0.0 copy-start.2
  2.1 1.0 copy-done.2
  3.1 0.0 copy-start.3
  3.1 1.0 copy-done.3
  4.2 0.0 copy-start.4
  4.2 1.0 copy-done.4
  5.2 0.0 copy-start.5
  5.2 1.0 copy-done.5
  6.3 0.0 copy-start.6
  6.3 1.0 copy-done.6
  7.3 0.0 copy-start.7
  7.3 0.7 copy-done.7
  8.0 0.0 copy-start.8
  8.0 0.7 copy-done.8
  8.7 195.0 %shard_map.91 = f32[1,3,64,16,128]{4,3,2,1,0:T(8,128)S(1)} custom-call(f32[1,64,16,128]{3,2,1,0:T(8,128)S(1)} %copy-done, f32[1,64,16,128]{3,2,1,0:T(8,128)S(1)} %copy-done.1, f32[1,64,16,128]{3,2,1,0:T(8,128)S(1)} %copy-done.2, f32[1,64,16,128]{3,2,1,0:T(8,128)S(1)} %copy-done.3, f32[1,64,16,128]{3,2,1,0:T(8,128)S(1)} %copy-done.4, ...), custom_call_target="tpu_custom_call" | custom-call | tf_op jit(solution)/shard_map/pallas_call | solution.py:283
  203.7 1.1 copy.11
Async XLA Ops:
  0.0 1.0 copy-start
  1.0 1.0 copy-start.1
  2.1 1.0 copy-start.2
  3.1 1.0 copy-start.3
  4.2 1.0 copy-start.4
  5.2 1.0 copy-start.5
  6.3 1.0 copy-start.6
  7.3 0.7 copy-start.7
  8.0 0.7 copy-start.8

commit v2 on v1

--- a/solution.py
+++ b/solution.py
@@ -10,18 +10,35 @@
 ITERS = 16
 OMEGA = 0.8
 MEMBRANE = 1.5
-CHUNKS = 4
+CHUNKS = 8
+UNROLL = 8
+COEF_UNROLL = 4
 MESH = pl.DeviceIdType.MESH
 f32 = jnp.float32
 
 
 def kernel(
     ngx, ngy, depth,
-    permeab, diffusivity, conductivity, velocity, overpotential, target, inlet, outlet, solid,
-    out,
+    permeab_hbm, diffusivity_hbm, conductivity_hbm, velocity_hbm, overpotential_hbm,
+    target_hbm, inlet_hbm, outlet_hbm, solid_hbm,
+    out_hbm,
+    permeab, diffusivity, conductivity, velocity, overpotential, target, inlet, outlet, solid, out,
     F, W, sx, hx, sy, hy, keep, extra, part, got_x, got_y,
-    send_sem, recv_sem, flow_send, flow_recv,
+    send_sem, recv_sem, flow_send, flow_recv, in_sem, out_sem,
 ):
+    loads = [
+        pltpu.make_async_copy(src, dst, in_sem.at[n])
+        for n, (src, dst) in enumerate(
+            (
+                (outlet_hbm, outlet), (inlet_hbm, inlet), (solid_hbm, solid),
+                (permeab_hbm, permeab), (diffusivity_hbm, diffusivity),
+                (conductivity_hbm, conductivity), (velocity_hbm, velocity),
+                (overpotential_hbm, overpotential), (target_hbm, target),
+            )
+        )
+    ]
+    for load in loads:
+        load.start()
     zc = depth // CHUNKS
     gx, gy, side = lax.axis_index("gx"), lax.axis_index("gy"), lax.axis_index("side")
     cells = float(16 * ngx * 128 * ngy)
@@ -57,14 +74,6 @@
             send_sem=flow_send.at[k, d], recv_sem=flow_recv.at[k, d],
             device_id={axis: peer}, device_id_type=MESH,
         )
-
-    tile = zero
-    for h in range(2):
-        rows = pl.ds(8 * h, 8)
-        tile = tile + outlet[0, rows].astype(f32) * velocity[0, depth - 1, rows]
-    part[0] = tile
-    for d in range(1, ngx):
-        flow_copy("gx", gx, ngx, d, part.at[0], got_x, True).start()
 
     has_lower = (gx > 0, gy > 0)
     has_upper = (gx < ngx - 1, gy < ngy - 1)
@@ -92,8 +101,10 @@
             @pl.when(can_send[d])
             def _(d=d):
                 halo_copy(p, d, c).start()
-        if membrane and c == 0:
-            halo_copy(p, 4, c).start()
+        if membrane:
+            @pl.when(c == 0)
+            def _():
+                halo_copy(p, 4, 0).start()
 
     def receive(p, c, membrane):
         for d in range(4):
@@ -104,10 +115,12 @@
             @pl.when(can_recv[d])
             def _(d=d):
                 halo_copy(p, d, c).wait_recv()
-        if membrane and c == 0:
-            copy = halo_copy(p, 4, c)
-            copy.wait_send()
-            copy.wait_recv()
+        if membrane:
+            @pl.when(c == 0)
+            def _():
+                copy = halo_copy(p, 4, 0)
+                copy.wait_send()
+                copy.wait_recv()
 
     def columns(p, c):
         lists = []
@@ -146,13 +159,17 @@
     def chunk_of(q, c, plane, unroll, store=True):
         def body(i, packed):
             packed = list(packed)
-            for u in range(unroll):
-                iz = i * unroll + u
-                for h in range(2):
-                    values = plane(iz, h)
+            spots = [(i * unroll + u, h) for u in range(unroll) for h in range(2)]
+            tiles = [plane(iz, h) for iz, h in spots]
+            for (iz, h), values in zip(spots, tiles):
+                for n, value in enumerate(values[3:]):
+                    W[n, c * zc + iz, pl.ds(8 * h, 8)] = value
+            for (iz, h), values in zip(spots, tiles):
+                for f in range(3):
                     if store:
-                        for f in range(3):
-                            packed[f] = put(q, c, f, iz, h, values[f], packed[f])
+                        packed[f] = put(q, c, f, iz, h, values[f], packed[f])
+                    else:
+                        out[f, c * zc + iz, pl.ds(8 * h, 8)] = values[f]
             return tuple(packed)
 
         packed = lax.fori_loop(0, zc // unroll, body, (zero, zero, zero))
@@ -160,14 +177,30 @@
             for f in range(3):
                 sy[q, c, f] = packed[f]
 
-    for c in range(CHUNKS):
-        def plane(iz, h, c=c):
+    for load in loads[2:6]:
+        load.wait()
+
+    def field_chunk(c, carry):
+        def plane(iz, h):
             z, rows = c * zc + iz, pl.ds(8 * h, 8)
             kp = permeab[0, z, rows] * (1.0 - 0.95 * solid[0, z, rows].astype(f32))
             return kp, diffusivity[0, z, rows], conductivity[0, z, rows]
 
-        chunk_of(0, c, plane, 2)
+        chunk_of(0, c, plane, 8)
         send(0, c, False)
+        return carry
+
+    lax.fori_loop(0, CHUNKS, field_chunk, 0)
+
+    for load in loads[:2] + loads[6:]:
+        load.wait()
+    tile = zero
+    for h in range(2):
+        rows = pl.ds(8 * h, 8)
+        tile = tile + outlet[0, rows].astype(f32) * velocity[0, depth - 1, rows]
+    part[0] = tile
+    for d in range(1, ngx):
+        flow_copy("gx", gx, ngx, d, part.at[0], got_x, True).start()
 
     for h in range(2):
         rows = pl.ds(8 * h, 8)
@@ -175,31 +208,20 @@
         keep[1, rows] = (1.0 - OMEGA) * (1.0 - inlet[0, rows].astype(f32))
         extra[rows] = zero
 
-    for c in range(CHUNKS):
-        if c == 0 and CHUNKS > 1:
-            total = part[0]
-            for d in range(1, ngx):
-                flow_copy("gx", gx, ngx, d, part.at[0], got_x, True).wait_send()
-                flow_copy("gx", gx, ngx, d, part.at[0], got_x, False).wait_recv()
-                total = total + got_x[lax.rem(gx + ngx - d, ngx)]
-            part[1] = total
-            for d in range(1, ngy):
-                flow_copy("gy", gy, ngy, d, part.at[1], got_y, True).start()
-        if c == CHUNKS - 1:
-            total = part[1]
-            for d in range(1, ngy):
-                flow_copy("gy", gy, ngy, d, part.at[1], got_y, True).wait_send()
-                flow_copy("gy", gy, ngy, d, part.at[1], got_y, False).wait_recv()
-                total = total + got_y[lax.rem(gy + ngy - d, ngy)]
-            outflow = jnp.sum(jnp.sum(total, axis=0, keepdims=True), axis=1, keepdims=True)
-            scale = jnp.broadcast_to((cells / 8.0) / (1.0 + outflow), (8, 128))
-            for h in range(2):
-                rows = pl.ds(8 * h, 8)
-                extra[rows] = outlet[0, rows].astype(f32) * scale
+    total = part[0]
+    for d in range(1, ngx):
+        flow_copy("gx", gx, ngx, d, part.at[0], got_x, True).wait_send()
+        flow_copy("gx", gx, ngx, d, part.at[0], got_x, False).wait_recv()
+        total = total + got_x[lax.rem(gx + ngx - d, ngx)]
+    part[1] = total
+    for d in range(1, ngy):
+        flow_copy("gy", gy, ngy, d, part.at[1], got_y, True).start()
+
+    def coef_chunk(c, carry):
         receive(0, c, False)
         cols = columns(0, c)
 
-        def plane(iz, h, c=c, cols=cols):
+        def plane(iz, h):
             z, rows = c * zc + iz, pl.ds(8 * h, 8)
             bottom = (z == 0).astype(f32)
             top = (z == depth - 1).astype(f32)
@@ -209,29 +231,42 @@
             g = jnp.full((8, 128), MEMBRANE, f32) * bottom
             source = target[0, z, rows] + top * extra[rows]
             free = 1.0 - top * inlet[0, rows].astype(f32)
-            for f, base in ((0, 0), (1, 7), (2, 15)):
+            rows_of = []
+            for f in range(3):
                 cen, near = around(0, c, f, iz, h, cols)
                 w = [0.5 * (cen + k) for k in near]
                 dsum = ((w[0] + w[1]) + (w[2] + w[3])) + (w[4] + w[5])
                 if f == 0:
                     factor = OMEGA / (dsum + 1.0)
-                    W[6, z, rows] = factor * vel
+                    more = [factor * vel]
                 elif f == 1:
                     factor = OMEGA * free / (dsum + vel + rate)
                     w[3] = w[3] + vel
                     start = factor * source
-                    W[13, z, rows] = start
-                    W[14, z, rows] = factor * rate
+                    more = [start, factor * rate]
                 else:
                     factor = OMEGA / (dsum + rate + g)
                     w[0] = w[0] * (1.0 - bottom) + g
-                    W[21, z, rows] = factor * rate
-                for n in range(6):
-                    W[base + n, z, rows] = factor * w[n]
-            return zero, start, zero
-
-        chunk_of(1, c, plane, 2)
+                    more = [factor * rate]
+                rows_of += [factor * k for k in w] + more
+            return (zero, start, zero, *rows_of)
+
+        chunk_of(1, c, plane, COEF_UNROLL)
         send(1, c, True)
+        return carry
+
+    lax.fori_loop(0, CHUNKS - 1, coef_chunk, 0)
+    total = part[1]
+    for d in range(1, ngy):
+        flow_copy("gy", gy, ngy, d, part.at[1], got_y, True).wait_send()
+        flow_copy("gy", gy, ngy, d, part.at[1], got_y, False).wait_recv()
+        total = total + got_y[lax.rem(gy + ngy - d, ngy)]
+    outflow = jnp.sum(jnp.sum(total, axis=0, keepdims=True), axis=1, keepdims=True)
+    scale = jnp.broadcast_to((cells / 8.0) / (1.0 + outflow), (8, 128))
+    for h in range(2):
+        rows = pl.ds(8 * h, 8)
+        extra[rows] = outlet[0, rows].astype(f32) * scale
+    lax.fori_loop(CHUNKS - 1, CHUNKS, coef_chunk, 0)
 
     def sweep_chunk(p, q, c, final):
         receive(p, c, True)
@@ -251,26 +286,39 @@
             p_new = mixed(0, pn) + ((1.0 - OMEGA) * pc + W[6, z, rows] * (cn[3] - cc))
             c_new = mixed(7, cn) + (keep[top, rows] * cc + (W[13, z, rows] + W[14, z, rows] * ec))
             e_new = mixed(15, en) + ((1.0 - OMEGA) * ec + W[21, z, rows] * cc)
-            if final:
-                out[0, 0, z, rows] = p_new
-                out[0, 1, z, rows] = c_new
-                out[0, 2, z, rows] = e_new
             return p_new, c_new, e_new
 
-        chunk_of(q, c, plane, 2, not final)
+        chunk_of(q, c, plane, UNROLL, not final)
         if not final:
             send(q, c, True)
 
     def sweep(t, carry):
         p = lax.rem(t, 2)
-        for c in range(CHUNKS):
+
+        def one(c, carry):
             sweep_chunk(p, 1 - p, c, False)
-        return carry
+            return carry
+
+        return lax.fori_loop(0, CHUNKS, one, carry)
 
     lax.fori_loop(1, ITERS - 1, sweep, 0)
     last = (ITERS - 1) % 2
-    for c in range(CHUNKS):
+
+    def store(c):
+        span = pl.ds(c * zc, zc)
+        return pltpu.make_async_copy(out.at[:, span], out_hbm.at[0, :, span], out_sem.at[c])
+
+    def finish(c, carry):
         sweep_chunk(last, 1 - last, c, True)
+        store(c).start()
+        return carry
+
+    def settle(c, carry):
+        store(c).wait()
+        return carry
+
+    lax.fori_loop(0, CHUNKS, finish, 0)
+    lax.fori_loop(0, CHUNKS, settle, 0)
 
 
 def solution(mesh):
@@ -279,13 +327,15 @@
     def local(*args):
         depth = args[0].shape[1]
         zc = depth // CHUNKS
-        vmem = pl.BlockSpec(memory_space=pltpu.VMEM)
+        hbm = pl.BlockSpec(memory_space=pl.ANY)
         return pl.pallas_call(
             functools.partial(kernel, ngx, ngy, depth),
             out_shape=jax.ShapeDtypeStruct((1, 3, depth, 16, 128), f32),
-            in_specs=[vmem] * 9,
-            out_specs=vmem,
-            scratch_shapes=[
+            in_specs=[hbm] * 9,
+            out_specs=hbm,
+            scratch_shapes=[pltpu.VMEM(a.shape, a.dtype) for a in args]
+            + [
+                pltpu.VMEM((3, depth, 16, 128), f32),
                 pltpu.VMEM((2, 3, depth + 2, 32, 128), f32),
                 pltpu.VMEM((22, depth, 16, 128), f32),
                 pltpu.VMEM((2, 2, CHUNKS, 3, zc, 128), f32),
@@ -301,6 +351,8 @@
                 pltpu.SemaphoreType.DMA((2, 5, CHUNKS)),
                 pltpu.SemaphoreType.DMA((2, max(ngx, ngy))),
                 pltpu.SemaphoreType.DMA((2, max(ngx, ngy))),
+                pltpu.SemaphoreType.DMA((9,)),
+                pltpu.SemaphoreType.DMA((CHUNKS,)),
             ],
             compiler_params=pltpu.CompilerParams(
                 collective_id=0, has_side_effects=True, vmem_limit_bytes=48 * 1024 * 1024

time: 205 us -> 74.5 us (0.36)
  Pallas kernels: 195 us -> 64.1 us
    pallas_call x1, Pallas kernels: 195 us -> 64.1 us  [local(): pl.pallas_call(functools.partial(kernel, ngx, ngy, depth), out_shape=jax....]
where the time goes in v2:
time: 74.5 us; the launch traced here: 74 us
  Pallas kernels  64.1 us (86%)
  local copies, waits for them, and re-layouts  9.83 us (13%)
    pallas_call x1, Pallas kernels, local(): pl.pallas_call(functools.partial(kernel, ngx, ngy, depth), out_shape=jax....  64.1 us
    unnamed x19, local copies, waits for them, and re-layouts  9.83 us

profile of v2, /device:TPU:0, one launch (start us, length us, event | category | flops | bytes accessed | tf_op | source)
XLA Modules:
  0.0 74.0 jit_solution(6524789855677590307)
XLA Ops:
  0.0 0.0 copy-start
  0.0 1.0 %copy-done = f32[1,64,16,128]{3,2,1,0:T(8,128)S(1)} copy-done((f32[1,64,16,128]{3,2,1,0:T(8,128)S(1)}, f32[1,64,16,128]{3,2,1,0:T(8,128)}, u32[]{:S(2)}) %copy-start) | copy-done | bytes 524312
  1.0 0.0 copy-start.1
  1.0 1.0 %copy-done.1 = f32[1,64,16,128]{3,2,1,0:T(8,128)S(1)} copy-done((f32[1,64,16,128]{3,2,1,0:T(8,128)S(1)}, f32[1,64,16,128]{3,2,1,0:T(8,128)}, u32[]{:S(2)}) %copy-start.1) | copy-done | bytes 524312
  2.1 0.0 copy-start.2
  2.1 1.0 %copy-done.2 = f32[1,64,16,128]{3,2,1,0:T(8,128)S(1)} copy-done((f32[1,64,16,128]{3,2,1,0:T(8,128)S(1)}, f32[1,64,16,128]{3,2,1,0:T(8,128)}, u32[]{:S(2)}) %copy-start.2) | copy-done | bytes 524312
  3.1 0.0 copy-start.3
  3.1 1.0 %copy-done.3 = f32[1,64,16,128]{3,2,1,0:T(8,128)S(1)} copy-done((f32[1,64,16,128]{3,2,1,0:T(8,128)S(1)}, f32[1,64,16,128]{3,2,1,0:T(8,128)}, u32[]{:S(2)}) %copy-start.3) | copy-done | bytes 524312
  4.2 0.0 copy-start.4
  4.2 1.0 %copy-done.4 = f32[1,64,16,128]{3,2,1,0:T(8,128)S(1)} copy-done((f32[1,64,16,128]{3,2,1,0:T(8,128)S(1)}, f32[1,64,16,128]{3,2,1,0:T(8,128)}, u32[]{:S(2)}) %copy-start.4) | copy-done | bytes 524312
  5.2 0.0 copy-start.5
  5.2 1.0 %copy-done.5 = f32[1,64,16,128]{3,2,1,0:T(8,128)S(1)} copy-done((f32[1,64,16,128]{3,2,1,0:T(8,128)S(1)}, f32[1,64,16,128]{3,2,1,0:T(8,128)}, u32[]{:S(2)}) %copy-start.5) | copy-done | bytes 524312
  6.3 0.0 copy-start.6
  6.3 1.0 %copy-done.6 = s32[1,64,16,128]{3,2,1,0:T(8,128)S(1)} copy-done((s32[1,64,16,128]{3,2,1,0:T(8,128)S(1)}, s32[1,64,16,128]{3,2,1,0:T(8,128)}, u32[]{:S(2)}) %copy-start.6) | copy-done | bytes 524312
  7.3 0.0 copy-start.7
  7.3 0.7 copy-done.7
  8.0 0.0 copy-start.8
  8.0 0.7 copy-done.8
  8.7 64.1 %shard_map.91 = f32[1,3,64,16,128]{4,3,2,1,0:T(8,128)S(1)} custom-call(f32[1,64,16,128]{3,2,1,0:T(8,128)S(1)} %copy-done, f32[1,64,16,128]{3,2,1,0:T(8,128)S(1)} %copy-done.1, f32[1,64,16,128]{3,2,1,0:T(8,128)S(1)} %copy-done.2, f32[1,64,16,128]{3,2,1,0:T(8,128)S(1)} %copy-done.3, f32[1,64,16,128]{3,2,1,0:T(8,128)S(1)} %copy-done.4, ...), custom_call_target="tpu_custom_call" | custom-call | tf_op jit(solution)/shard_map/pallas_call | solution.py:331
  72.8 1.1 %copy.11 = f32[1,3,64,16,128]{4,3,2,1,0:T(8,128)} copy(f32[1,3,64,16,128]{4,3,2,1,0:T(8,128)S(1)} %shard_map.91) | data formatting | bytes 3145728
Async XLA Ops:
  0.0 1.0 %copy-start = (f32[1,64,16,128]{3,2,1,0:T(8,128)S(1)}, f32[1,64,16,128]{3,2,1,0:T(8,128)}, u32[]{:S(2)}) copy-start(f32[1,64,16,128]{3,2,1,0:T(8,128)} %permeab_hbm.1) | copy-start | bytes 1572868
  1.0 1.0 %copy-start.1 = (f32[1,64,16,128]{3,2,1,0:T(8,128)S(1)}, f32[1,64,16,128]{3,2,1,0:T(8,128)}, u32[]{:S(2)}) copy-start(f32[1,64,16,128]{3,2,1,0:T(8,128)} %diffusivity_hbm.1) | copy-start | bytes 1572868
  2.1 1.0 %copy-start.2 = (f32[1,64,16,128]{3,2,1,0:T(8,128)S(1)}, f32[1,64,16,128]{3,2,1,0:T(8,128)}, u32[]{:S(2)}) copy-start(f32[1,64,16,128]{3,2,1,0:T(8,128)} %conductivity_hbm.1) | copy-start | bytes 1572868
  3.1 1.0 %copy-start.3 = (f32[1,64,16,128]{3,2,1,0:T(8,128)S(1)}, f32[1,64,16,128]{3,2,1,0:T(8,128)}, u32[]{:S(2)}) copy-start(f32[1,64,16,128]{3,2,1,0:T(8,128)} %velocity_hbm.1) | copy-start | bytes 1572868
  4.2 1.0 %copy-start.4 = (f32[1,64,16,128]{3,2,1,0:T(8,128)S(1)}, f32[1,64,16,128]{3,2,1,0:T(8,128)}, u32[]{:S(2)}) copy-start(f32[1,64,16,128]{3,2,1,0:T(8,128)} %overpotential_hbm.1) | copy-start | bytes 1572868
  5.2 1.0 %copy-start.5 = (f32[1,64,16,128]{3,2,1,0:T(8,128)S(1)}, f32[1,64,16,128]{3,2,1,0:T(8,128)}, u32[]{:S(2)}) copy-start(f32[1,64,16,128]{3,2,1,0:T(8,128)} %target_hbm.1) | copy-start | bytes 1572868
  6.3 1.0 %copy-start.6 = (s32[1,64,16,128]{3,2,1,0:T(8,128)S(1)}, s32[1,64,16,128]{3,2,1,0:T(8,128)}, u32[]{:S(2)}) copy-start(s32[1,64,16,128]{3,2,1,0:T(8,128)} %solid_hbm.1) | copy-start | bytes 1572868
  7.3 0.7 copy-start.7
  8.0 0.7 copy-start.8
